TPU v7x, 32 devices: a whole 2x2x4 slice. The times are simulated.
32 devices in a mesh: groups: 2 (over y), atoms: 4 (over z), kvec: 2 (over x), rep: 2 (over core).
Axes of the slice: x: 2, y: 2, z: 4, core: 2. Of those that a mesh axis runs over, the one named last changes fastest.
Arguments:
- positions: float32 [4, 3, 8192], P(('groups', 'rep'), None, 'atoms'), parts along dimension 0, may hold values from 0 to 1
- features: bfloat16 [4, 8192, 256], P(('groups', 'rep'), 'atoms'), parts along dimension 0
- species: int32 [4, 8192], P(('groups', 'rep'), 'atoms'), parts along dimension 0, may hold values from 0 to 7
- cell_length: float32 [4], P(('groups', 'rep')), parts along dimension 0, may hold values from 40 to 60
- energy_ref: float32 [4], P(('groups', 'rep')), parts along dimension 0, may hold values from -12 to -6
- miller_index: int32 [3, 2048], P(None, 'kvec'), may hold values from -8 to 8, as said below
- weight_in: bfloat16 [256, 512], replicated, may hold values from -0.375 to 0.375
- weight_mid: bfloat16 [512, 512], replicated, may hold values from -0.25 to 0.25
- weight_out: bfloat16 [512, 32], replicated, may hold values from -0.25 to 0.25
- species_bias: float32 [8, 512], replicated, may hold values from -3 to 3
Outputs:
- potential: float32 [4, 8192, 32], P(('groups', 'rep'), ('atoms', 'kvec')), parts along dimension 0
- energy: float32 [4], P(('groups', 'rep')), parts along dimension 0
- grad_in: float32 [512, 512], P('groups'), parts along dimension 0
- grad_mid: float32 [1024, 512], P('groups'), parts along dimension 0
- grad_out: float32 [1024, 32], P('groups'), parts along dimension 0
- grad_bias: float32 [16, 512], P('groups'), parts along dimension 0
There are 2 independent parts, one for each index of `groups`. A program takes and returns all parts, laid end to end along the dimension named above; an argument that names none is the same for every part. Nothing has to cross between parts.
Inputs may be any that keep to these rules, and one draw needn't show every extreme that they name: No column of miller_index is all zeros.
All inputs are finite; a program needn't handle non-finite values.
Results may differ from a plain program's by a relative error of at most 0.0046.
Values may be sent and summed in bfloat16 or wider, within the bound.
A program may use at most 64 MiB of HBM per device.

v0:
```python
import math
import jax
import jax.numpy as jnp
from jax import lax
from jax.sharding import PartitionSpec as P

KVECS = 2048
TWO_PI = 2.0 * math.pi
HIGHEST = lax.Precision.HIGHEST


def phase_tiles(coord_rows, miller_float):
    phase_turns = (
        coord_rows[0][:, None] * miller_float[0][None, :]
        + coord_rows[1][:, None] * miller_float[1][None, :]
        + coord_rows[2][:, None] * miller_float[2][None, :]
    )
    phase_angle = TWO_PI * phase_turns
    return jnp.concatenate([jnp.cos(phase_angle), jnp.sin(phase_angle)], axis=1).astype(
        jnp.bfloat16
    )


def wave_weights(miller_float, cell_size, atoms_total):
    index_square = (
        miller_float[0] * miller_float[0]
        + miller_float[1] * miller_float[1]
        + miller_float[2] * miller_float[2]
    )
    factor = TWO_PI / cell_size
    wave_square = index_square * (factor * factor)
    decay_base = jnp.exp(-0.5 * wave_square) / wave_square * (1.0 / math.sqrt(atoms_total * KVECS))
    return jnp.concatenate([decay_base, decay_base])


def contract_rows(left_rows, right_rows):
    return lax.dot_general(
        left_rows, right_rows, (((0,), (0,)), ((), ())), preferred_element_type=jnp.float32
    )


def silu_slope(linear):
    sigmoid_value = jax.nn.sigmoid(linear)
    return sigmoid_value * (1.0 + linear * (1.0 - sigmoid_value))


def forward(atom_features, atom_species, weight_in, weight_mid, weight_out, species_bias):
    kinds = jnp.arange(species_bias.shape[0], dtype=jnp.int32)
    onehot = (atom_species[:, None] == kinds[None, :]).astype(jnp.float32)
    bias_rows = jnp.dot(onehot, species_bias, precision=HIGHEST, preferred_element_type=jnp.float32)
    linear_one = jnp.dot(atom_features, weight_in, preferred_element_type=jnp.float32) + bias_rows
    hidden_one = jax.nn.silu(linear_one).astype(jnp.bfloat16)
    linear_two = jnp.dot(hidden_one, weight_mid, preferred_element_type=jnp.float32)
    hidden_two = jax.nn.silu(linear_two).astype(jnp.bfloat16)
    charges = jnp.dot(hidden_two, weight_out, preferred_element_type=jnp.float32).astype(
        jnp.bfloat16
    )
    return (onehot, linear_one, hidden_one, linear_two, hidden_two, charges)


def backward(
    atom_features,
    onehot,
    linear_one,
    hidden_one,
    linear_two,
    hidden_two,
    grad_charges,
    weight_mid,
    weight_out,
):
    grad_out = contract_rows(hidden_two, grad_charges)
    back_two = lax.dot_general(
        grad_charges, weight_out, (((1,), (1,)), ((), ())), preferred_element_type=jnp.float32
    )
    grad_two = (back_two * silu_slope(linear_two)).astype(jnp.bfloat16)
    grad_mid = contract_rows(hidden_one, grad_two)
    back_one = lax.dot_general(
        grad_two, weight_mid, (((1,), (1,)), ((), ())), preferred_element_type=jnp.float32
    )
    grad_one = (back_one * silu_slope(linear_one)).astype(jnp.bfloat16)
    grad_in = contract_rows(atom_features, grad_one)
    grad_bias = contract_rows(onehot.astype(jnp.bfloat16), grad_one)
    return (grad_in, grad_mid, grad_out, grad_bias)


def body(
    positions,
    features,
    species,
    cell_length,
    energy_ref,
    miller_index,
    weight_in,
    weight_mid,
    weight_out,
    species_bias,
):
    block_rows = positions.shape[2]
    kvec_count = miller_index.shape[1]
    channels = weight_out.shape[1]
    atoms_total = block_rows * lax.axis_size("atoms")
    quarter = block_rows // lax.axis_size("kvec")
    own_first = lax.axis_index("kvec") * quarter
    miller_float = miller_index.astype(jnp.float32)
    column_weights = wave_weights(miller_float, cell_length[0], atoms_total)
    coords = positions[0]
    step_rows = math.gcd(block_rows, 512)
    stored = jnp.concatenate(
        [
            phase_tiles(lax.slice_in_dim(coords, offset, offset + step_rows, axis=1), miller_float)
            for offset in range(0, block_rows, step_rows)
        ],
        axis=0,
    )

    def tile_rows(first_row, row_count):
        return lax.dynamic_slice_in_dim(stored, first_row, row_count, 0)

    zero_panels = jnp.zeros((channels, 2 * kvec_count), jnp.float32)
    own_features = features[0]
    own_species = species[0]
    onehot, linear_one, hidden_one, linear_two, hidden_two, charges = forward(
        own_features, own_species, weight_in, weight_mid, weight_out, species_bias
    )
    running = zero_panels
    row_count = charges.shape[0]
    piece_rows = math.gcd(row_count, 512)
    for inner_start in range(0, row_count, piece_rows):
        phase_rows = tile_rows(0 + inner_start, piece_rows)
        running = running + contract_rows(
            lax.slice_in_dim(charges, inner_start, inner_start + piece_rows, axis=0), phase_rows
        )
    summed = lax.psum(running, "atoms")
    energy_sum = lax.psum(jnp.sum(summed * summed * column_weights[None, :]).reshape(1), "kvec")
    weighted = (summed * column_weights[None, :]).astype(jnp.bfloat16)
    energy = energy_sum / atoms_total
    piece_rows = math.gcd(block_rows, 512)
    pieces = []
    for inner_start in range(0, block_rows, piece_rows):
        phase_rows = tile_rows(0 + inner_start, piece_rows)
        pieces.append(
            lax.dot_general(
                phase_rows, weighted, (((1,), (1,)), ((), ())), preferred_element_type=jnp.float32
            )
        )
    used_potential = lax.psum(jnp.concatenate(pieces, axis=0), "kvec")
    own_potential = lax.dynamic_slice_in_dim(used_potential, own_first, quarter, 0)
    loss_scale = (energy[0] - energy_ref[0]) * (2.0 / atoms_total)
    grad_charges = (loss_scale * used_potential).astype(jnp.bfloat16)
    local_in, local_mid, local_out, local_bias = backward(
        own_features,
        onehot,
        linear_one,
        hidden_one,
        linear_two,
        hidden_two,
        grad_charges,
        weight_mid,
        weight_out,
    )
    grad_in, grad_mid, grad_out, grad_bias = lax.psum(
        (local_in, local_mid, local_out, local_bias), ("atoms", "rep")
    )
    return (own_potential[None], energy, grad_in, grad_mid, grad_out, grad_bias)


def solution(mesh):
    placed = (
        P(("groups", "rep"), None, "atoms"),
        P(("groups", "rep"), "atoms", None),
        P(("groups", "rep"), "atoms"),
        P(("groups", "rep")),
        P(("groups", "rep")),
        P(None, "kvec"),
        P(),
        P(),
        P(),
        P(),
    )
    return jax.shard_map(
        body,
        mesh=mesh,
        in_specs=placed,
        out_specs=(
            P(("groups", "rep"), ("atoms", "kvec"), None),
            P(("groups", "rep")),
            P("groups", None),
            P("groups", None),
            P("groups", None),
            P("groups", None),
        ),
        check_vma=False,
    )
```

profile of v0, /device:TPU:0, one launch (start us, length us, event | category | flops | bytes accessed | tf_op | source)
XLA Modules:
  0.0 213.0 jit_solution(59138224484041995)
XLA Ops:
  7.2 0.0 copy-start
  7.2 0.0 all-reduce.5.cloned.1.call-start
  7.2 0.8 convert_element_type.34
  8.0 0.8 copy.19
  8.8 0.0 copy-done
  8.8 0.0 copy-start.16
  8.8 0.0 copy-start.19
  8.9 1.7 fusion.6
  10.5 0.0 copy-done.16
  10.5 0.0 copy-done.19
  10.6 0.0 copy-start.17
  10.6 4.2 %multiply_convert_fusion.3 = (bf16[2048,512]{1,0:T(8,128)(2,1)S(1)}, f32[2048,512]{1,0:T(8,128)}) fusion(f32[2048,512]{1,0:T(8,128)S(1)} %fusion.6, f32[8,512]{1,0:T(8,128)S(1)} %copy-done.19, s32[2048]{0:T(1024)S(1)} %bitcast.56), kind=kOutput, calls=%fused_computation.4 | convolution fusion | flops 106971136 | bytes 10510336 | tf_op jit(solution)/shard_map/dot_general | solution.py:50
  14.8 3.8 %multiply_convert_fusion.2 = (bf16[2048,512]{1,0:T(8,128)(2,1)S(1)}, f32[2048,512]{1,0:T(8,128)}) fusion(bf16[2048,512]{1,0:T(8,128)(2,1)S(1)} %get-tuple-element.46, bf16[512,512]{1,0:T(8,128)(2,1)S(1)} %copy-done.17), kind=kOutput, calls=%fused_computation.2 | convolution fusion | flops 1078984704 | bytes 8912896 | tf_op jit(solution)/shard_map/dot_general | solution.py:53
  18.5 0.7 convolution_convert_fusion
  19.2 33.6 %cosine_convert_fusion = (bf16[512,1024]{1,0:T(8,128)(2,1)S(1)}, bf16[512,1024]{1,0:T(8,128)(2,1)S(1)}, bf16[512,1024]{1,0:T(8,128)(2,1)S(1)}, bf16[512,1024]{1,...) fusion(f32[512]{0:T(512)S(1)} %bitcast.59, ...), kind=kLoop, calls=%fused_computation.16 | loop fusion | flops 16777216 | bytes 8425472 | tf_op jit(solution)/shard_map/convert
  52.8 0.0 copy-done.1
  52.8 0.0 copy-start.3
  52.8 0.0 copy-start.5
  52.8 0.0 copy-start.7
  52.9 0.0 copy-start.9
  52.9 0.0 copy-start.11
  52.9 0.0 copy-start.12
  52.9 0.5 fusion.4
  53.4 0.5 convolution_add_fusion.3
  53.8 0.0 copy-done.3
  53.9 0.3 copy-done.5
  54.2 0.3 copy-done.7
  54.5 0.3 copy-done.9
  54.8 0.5 convolution_add_fusion.2
  55.2 0.0 copy-done.11
  55.2 0.2 copy-done.12
  55.5 1.2 convolution_add_fusion.1
  56.7 0.0 all-reduce.5.cloned.1.call-update
  56.7 0.0 all-reduce.7.cloned.1.call-start
  57.5 37.4 %all-reduce.5.cloned.1.call-done = f32[32,2048]{1,0:T(8,128)} async-done(((f32[32,2048]{1,0:T(8,128)}), f32[32,2048]{1,0:T(8,128)}) %all-reduce.5.cloned.1.call-update) | async-done | bytes 262160 | tf_op jit(solution)/shard_map/psum | solution.py:134
  94.8 1.8 multiply_reduce_fusion
  96.6 2.3 %fusion = f32[512,32]{0,1:T(8,128)S(1)} fusion(bf16[32,2048]{1,0:T(8,128)(2,1)S(1)} %get-tuple-element.16, bf16[512,1024]{1,0:T(8,128)(2,1)} %copy-done.12, bf16[512,1024]{1,0:T(8,128)(2,1)} %copy-done.11), kind=kOutput, calls=%fused_computation.27 | convolution fusion | flops 71303168 | bytes 2293760 | tf_op jit(solution)/shard_map/dot_general | solution.py:143
  98.9 0.0 copy-done.8
  98.9 0.7 fusion.1
  99.6 0.5 copy-done.4
  100.1 0.3 copy-done.6
  100.4 0.7 fusion.2
  101.2 0.7 fusion.3
  101.9 0.7 pad_maximum_fusion.12
  102.7 0.0 all-reduce.7.cloned.1.call-update
  102.7 0.0 all-reduce.9.cloned.1.call-start
  103.4 5.6 %psum.51 = f32[1]{0:T(128)} all-reduce(f32[1]{0:T(128)} %bitcast.19), channel_id=1, replica_groups=mesh['groups'=2,'atoms'=4,'kvec'=2,'rep'=2] {'kvec'}, use_global_device_ids=true, to_apply=%region_3.4 | all-reduce | flops 1 | bytes 8 | tf_op jit(solution)/shard_map/psum | solution.py:135
  109.6 16.1 %all-reduce.7.cloned.1.call-done = f32[2048,32]{0,1:T(8,128)} async-done(((f32[2048,32]{0,1:T(8,128)}), f32[2048,32]{0,1:T(8,128)}) %all-reduce.7.cloned.1.call-update) | async-done | bytes 262160 | tf_op jit(solution)/shard_map/psum | solution.py:147
  125.8 4.2 %multiply_convert_fusion.1 = bf16[2048,512]{1,0:T(8,128)(2,1)S(1)} fusion(f32[2048,512]{1,0:T(8,128)} %get-tuple-element.49, bf16[512,32]{0,1:T(8,128)(2,1)S(1)} %copy-done.15, f32[2048,32]{0,1:T(8,128)} %all-reduce.7.cloned.1.call-done, f32[]{:T(128)} %bitcast.20), kind=kOutput, calls=%fused_computation.1 | convolution fusion | flops 76677120 | bytes 6586372 | tf_op jit(solution)/shard_map/dot_general | solution.py:73
  129.9 0.0 copy-start.18
  130.0 2.3 %fusion.26 = f32[512,512]{1,0:T(8,128)} fusion(bf16[2048,512]{1,0:T(8,128)(2,1)S(1)} %copy-done.21, bf16[2048,512]{1,0:T(8,128)(2,1)S(1)} %multiply_convert_fusion.1), kind=kOutput, calls=%fused_computation.64 | convolution fusion | flops 1073741824 | bytes 5242880 | tf_op jit(solution)/shard_map/dot_general | solution.py:37
  132.2 0.3 copy-done.22
  132.5 2.3 %multiply_convert_fusion = bf16[2048,512]{1,0:T(8,128)(2,1)S(1)} fusion(f32[2048,512]{1,0:T(8,128)S(1)} %copy-done.22, bf16[2048,512]{1,0:T(8,128)(2,1)S(1)} %multiply_convert_fusion.1, bf16[512,512]{1,0:T(8,128)(2,1)S(1)} %copy-done.18), kind=kOutput, calls=%fused_computation | convolution fusion | flops 1083179008 | bytes 8912896 | tf_op jit(solution)/shard_map/dot_general | solution.py:78
  134.9 1.5 convolution_bitcast_fusion
  136.5 0.0 copy-done.2
  136.5 1.1 fusion.11
  137.6 0.0 all-reduce.9.cloned.1.call-update
  137.6 0.8 fusion.8
  138.4 29.5 %psum.55 = f32[8,512]{1,0:T(8,128)} all-reduce(f32[8,512]{1,0:T(8,128)S(1)} %fusion.8), channel_id=1, replica_groups=mesh['groups'=2,'atoms'=4,'kvec'=2,'rep'=2] {'atoms','rep'}, use_global_device_ids=true, to_apply=%region_7.8 | all-reduce | flops 4096 | bytes 32768 | tf_op jit(solution)/shard_map/psum | solution.py:162
  167.9 0.7 dynamic-slice_bitcast_fusion
  168.6 31.8 %all-reduce.9.cloned.1.call-done = (f32[256,512]{0,1:T(8,128)}, f32[512,512]{1,0:T(8,128)}, f32[512,32]{0,1:T(8,128)}) async-done(((f32[256,512]{0,1:T(8,128)}, f32[512,512]{1,0:T(8,128)}, f32[512,32]{0,1:T(8,128)}), (f32[256,512]{0,1:T(8,128)}, f32[512,512]{1,0:T(8,128)}, f32[512,32]{0,1:T(8,128)})) %all-reduce.9.cloned.1.call-update) | async-done | bytes 1638416 | tf_op jit(solution)/shard_map/psum | solution.py:162
  200.3 2.1 copy.16
  202.4 2.3 %copy.27 = f32[512,512]{1,0:T(8,128)} copy(f32[512,512]{1,0:T(8,128)} %get-tuple-element.53) | data formatting | bytes 2097152
  204.7 0.6 copy.28
  (24 shorter events, 0.1 us)
Async XLA Ops:
  7.2 1.7 copy-start
  7.2 87.7 %all-reduce.5.cloned.1.call-start = ((), (), s32[]{:S(2)}) async-start(), calls=%async_computation | async-start | bytes 524288 | tf_op jit(solution)/shard_map/psum | solution.py:134
  8.8 1.7 copy-start.16
  8.8 1.7 copy-start.19
  10.6 4.2 %copy-start.17 = (bf16[512,512]{1,0:T(8,128)(2,1)S(1)}, bf16[512,512]{1,0:T(8,128)(2,1)}, u32[]{:S(2)}) copy-start(bf16[512,512]{1,0:T(8,128)(2,1)} %param.17) | copy-start | bytes 1572868
  14.8 3.8 %copy-start.20 = (bf16[2048,512]{1,0:T(8,128)(2,1)}, bf16[2048,512]{1,0:T(8,128)(2,1)S(1)}, u32[]{:S(2)}) copy-start(bf16[2048,512]{1,0:T(8,128)(2,1)S(1)} %get-tuple-element.46) | copy-start | bytes 6291460
  14.8 3.8 %copy-start.15 = (bf16[512,32]{0,1:T(8,128)(2,1)S(1)}, bf16[512,32]{0,1:T(8,128)(2,1)}, u32[]{:S(2)}) copy-start(bf16[512,32]{0,1:T(8,128)(2,1)} %param.18) | copy-start | bytes 98308
  18.5 34.3 %copy-start.1 = (bf16[2048,512]{1,0:T(8,128)(2,1)}, bf16[2048,512]{1,0:T(8,128)(2,1)S(1)}, u32[]{:S(2)}) copy-start(bf16[2048,512]{1,0:T(8,128)(2,1)S(1)} %get-tuple-element.48) | copy-start | bytes 6291460
  52.8 1.0 copy-start.3
  52.8 1.3 copy-start.5
  52.8 1.6 copy-start.7
  52.9 1.9 copy-start.9
  52.9 2.4 %copy-start.11 = (bf16[512,1024]{1,0:T(8,128)(2,1)}, bf16[512,1024]{1,0:T(8,128)(2,1)S(1)}, u32[]{:S(2)}) copy-start(bf16[512,1024]{1,0:T(8,128)(2,1)S(1)} %get-tuple-element.29) | copy-start | bytes 3145732
  52.9 2.6 %copy-start.12 = (bf16[512,1024]{1,0:T(8,128)(2,1)}, bf16[512,1024]{1,0:T(8,128)(2,1)S(1)}, u32[]{:S(2)}) copy-start(bf16[512,1024]{1,0:T(8,128)(2,1)S(1)} %get-tuple-element.30) | copy-start | bytes 3145732
  56.7 69.1 %all-reduce.7.cloned.1.call-start = ((), (), s32[]{:S(2)}) async-start(), calls=%async_computation.1 | async-start | bytes 524288 | tf_op jit(solution)/shard_map/psum | solution.py:147
  94.8 4.1 %copy-start.8 = (bf16[512,1024]{1,0:T(8,128)(2,1)S(1)}, bf16[512,1024]{1,0:T(8,128)(2,1)}, u32[]{:S(2)}) copy-start(bf16[512,1024]{1,0:T(8,128)(2,1)} %copy-done.7) | copy-start | bytes 3145732
  94.8 4.1 %copy-start.10 = (bf16[512,1024]{1,0:T(8,128)(2,1)S(1)}, bf16[512,1024]{1,0:T(8,128)(2,1)}, u32[]{:S(2)}) copy-start(bf16[512,1024]{1,0:T(8,128)(2,1)} %copy-done.9) | copy-start | bytes 3145732
  98.9 1.2 copy-start.4
  98.9 1.5 copy-start.6
  102.7 97.7 %all-reduce.9.cloned.1.call-start = ((), (), s32[]{:S(2)}) async-start(), calls=%async_computation.2 | async-start | bytes 3276800 | tf_op jit(solution)/shard_map/psum | solution.py:162
  125.8 4.2 %copy-start.21 = (bf16[2048,512]{1,0:T(8,128)(2,1)S(1)}, bf16[2048,512]{1,0:T(8,128)(2,1)}, u32[]{:S(2)}) copy-start(bf16[2048,512]{1,0:T(8,128)(2,1)} %copy-done.20) | copy-start | bytes 6291460
  129.9 2.3 %copy-start.18 = (bf16[512,512]{1,0:T(8,128)(2,1)S(1)}, bf16[512,512]{1,0:T(8,128)(2,1)}, u32[]{:S(2)}) copy-start(bf16[512,512]{1,0:T(8,128)(2,1)} %param.17) | copy-start | bytes 1572868
  130.0 2.6 %copy-start.22 = (f32[2048,512]{1,0:T(8,128)S(1)}, f32[2048,512]{1,0:T(8,128)}, u32[]{:S(2)}) copy-start(f32[2048,512]{1,0:T(8,128)} %get-tuple-element.47) | copy-start | bytes 12582916
  134.9 1.6 copy-start.2
  134.9 1.6 copy-start.13
  200.3 4.3 %copy-start.14 = (f32[512,32]{0,1:T(8,128)S(1)}, f32[512,32]{0,1:T(8,128)}, u32[]{:S(2)}) copy-start(f32[512,32]{0,1:T(8,128)} %get-tuple-element.54) | copy-start | bytes 196612
Sparse Core Ops, SparseCore 0:
  56.8 37.9 all-reduce.4
  102.8 22.9 all-reduce.6
  137.7 62.5 all-reduce.8
where the time goes:
time: 213 us
  waiting for transfers between devices  85.4 us (40%)
  other arithmetic  36.9 us (17%)
  blocking collectives  35.1 us (16%)
  matrix products  29.5 us (14%)
  between operations  17.1 us (8%)
  local copies, waits for them, and re-layouts  8.84 us (4%)
    psum x1, waiting for transfers between devices, body(): summed = lax.psum(running, 'atoms')  37.4 us
    another operation x1, other arithmetic  33.6 us
    psum x1, waiting for transfers between devices, body(): lax.psum((local_in, local_mid, local_out, local_bias), ('atoms', 'rep'))  31.8 us
    psum x1, blocking collectives, body(): lax.psum((local_in, local_mid, local_out, local_bias), ('atoms', 'rep'))  29.5 us
    psum x1, waiting for transfers between devices, body(): used_potential = lax.psum(jnp.concatenate(pieces, axis=0), 'kvec')  16.1 us
    dot_general x8, matrix products, contract_rows(): lax.dot_general(left_rows, right_rows, (((0,), (0,)), ((), ())), preferre...  8.23 us
    unnamed x50, local copies, waits for them, and re-layouts  8.15 us
    psum x1, blocking collectives, body(): lax.psum(jnp.sum(summed * summed * column_weights[None, :]).reshape(1), '...  5.58 us
  transfers between devices with their start and end apart: 3, of which 3 were waited for; matrix products, arithmetic and copies ran while one was open for 1% of the time, Pallas kernels for 0%

commit v1 on v0

--- a/solution.py
+++ b/solution.py
@@ -160,7 +160,7 @@
         weight_out,
     )
     grad_in, grad_mid, grad_out, grad_bias = lax.psum(
-        (local_in, local_mid, local_out, local_bias), ("atoms", "rep")
+        lax.psum((local_in, local_mid, local_out, local_bias), "rep"), "atoms"
     )
     return (own_potential[None], energy, grad_in, grad_mid, grad_out, grad_bias)
 

time: 213 us -> 248 us (1.16)
  waiting for transfers between devices: 85.4 us -> 125 us
  blocking collectives: 35.1 us -> 29.3 us
    psum x1 -> x2, waiting for transfers between devices: 31.8 us -> 71.8 us  [the longest x1 51 us: body(): lax.psum(lax.psum((local_in, local_mid, local_out, local_bias), 'rep'), '...]
    psum x1 -> x2, blocking collectives: 29.5 us -> 23.8 us  [the longest x1 20.4 us: body(): lax.psum(lax.psum((local_in, local_mid, local_out, local_bias), 'rep'), '...]
  transfers between devices with their start and end apart: 3 -> 4, of which waited for: 3 -> 4; matrix products, arithmetic and copies ran while one was open for 1% -> 1% of each run, Pallas kernels for 0% -> 0%
where the time goes in v1:
time: 248 us; the launch traced here: 247 us
  waiting for transfers between devices  125 us (50%)
  other arithmetic  36.9 us (15%)
  matrix products  29.6 us (12%)
  blocking collectives  29.3 us (12%)
  between operations  17.2 us (7%)
  local copies, waits for them, and re-layouts  8.84 us (4%)
    psum x1, waiting for transfers between devices, body(): lax.psum(lax.psum((local_in, local_mid, local_out, local_bias), 'rep'), '...  51 us
    psum x1, waiting for transfers between devices, body(): summed = lax.psum(running, 'atoms')  37.4 us
    another operation x1, other arithmetic  33.6 us
    psum x1, waiting for transfers between devices, body(): lax.psum((local_in, local_mid, local_out, local_bias), 'rep')  20.8 us
    psum x1, blocking collectives, body(): lax.psum(lax.psum((local_in, local_mid, local_out, local_bias), 'rep'), '...  20.4 us
    psum x1, waiting for transfers between devices, body(): used_potential = lax.psum(jnp.concatenate(pieces, axis=0), 'kvec')  16.1 us
    dot_general x8, matrix products, contract_rows(): lax.dot_general(left_rows, right_rows, (((0,), (0,)), ((), ())), preferre...  8.23 us
    unnamed x50, local copies, waits for them, and re-layouts  8.14 us
  transfers between devices with their start and end apart: 4, of which 4 were waited for; matrix products, arithmetic and copies ran while one was open for 1% of the time, Pallas kernels for 0%

profile of v1, /device:TPU:0, one launch (start us, length us, event | category | flops | bytes accessed | tf_op | source)
XLA Modules:
  0.0 247.3 jit_solution(17283530213473628190)
XLA Ops:
  7.2 0.0 copy-start
  7.2 0.0 all-reduce.7.cloned.1.call-start
  7.2 0.8 convert_element_type.34
  8.0 0.8 copy.19
  8.8 0.0 copy-done
  8.8 0.0 copy-start.16
  8.8 0.0 copy-start.19
  8.9 1.7 fusion.6
  10.5 0.0 copy-done.16
  10.5 0.0 copy-done.19
  10.6 0.0 copy-start.17
  10.6 4.2 %multiply_convert_fusion.3 = (bf16[2048,512]{1,0:T(8,128)(2,1)S(1)}, f32[2048,512]{1,0:T(8,128)}) fusion(f32[2048,512]{1,0:T(8,128)S(1)} %fusion.6, f32[8,512]{1,0:T(8,128)S(1)} %copy-done.19, s32[2048]{0:T(1024)S(1)} %bitcast.56), kind=kOutput, calls=%fused_computation.4 | convolution fusion | flops 106971136 | bytes 10510336 | tf_op jit(solution)/shard_map/dot_general | solution.py:50
  14.8 0.0 copy-done.17
  14.8 3.8 %multiply_convert_fusion.2 = (bf16[2048,512]{1,0:T(8,128)(2,1)S(1)}, f32[2048,512]{1,0:T(8,128)}) fusion(bf16[2048,512]{1,0:T(8,128)(2,1)S(1)} %get-tuple-element.49, bf16[512,512]{1,0:T(8,128)(2,1)S(1)} %copy-done.17), kind=kOutput, calls=%fused_computation.2 | convolution fusion | flops 1078984704 | bytes 8912896 | tf_op jit(solution)/shard_map/dot_general | solution.py:53
  18.6 0.7 convolution_convert_fusion
  19.3 33.6 %cosine_convert_fusion = (bf16[512,1024]{1,0:T(8,128)(2,1)S(1)}, bf16[512,1024]{1,0:T(8,128)(2,1)S(1)}, bf16[512,1024]{1,0:T(8,128)(2,1)S(1)}, bf16[512,1024]{1,...) fusion(f32[512]{0:T(512)S(1)} %bitcast.59, ...), kind=kLoop, calls=%fused_computation.16 | loop fusion | flops 16777216 | bytes 8425472 | tf_op jit(solution)/shard_map/convert
  52.8 0.0 copy-done.1
  52.9 0.0 copy-start.12
  52.9 0.5 fusion.4
  53.4 0.5 convolution_add_fusion.3
  53.8 0.0 copy-done.3
  53.9 0.3 copy-done.5
  54.2 0.3 copy-done.7
  54.5 0.3 copy-done.9
  54.8 0.5 convolution_add_fusion.2
  55.3 0.0 copy-done.11
  55.3 0.2 copy-done.12
  55.5 1.2 convolution_add_fusion.1
  56.7 0.0 all-reduce.7.cloned.1.call-update
  56.7 0.0 all-reduce.9.cloned.1.call-start
  57.5 37.4 %all-reduce.7.cloned.1.call-done = f32[32,2048]{1,0:T(8,128)} async-done(((f32[32,2048]{1,0:T(8,128)}), f32[32,2048]{1,0:T(8,128)}) %all-reduce.7.cloned.1.call-update) | async-done | bytes 262160 | tf_op jit(solution)/shard_map/psum | solution.py:134
  94.8 1.8 multiply_reduce_fusion
  96.6 2.3 fusion
  98.9 0.0 copy-done.8
  98.9 0.7 fusion.1
  99.7 0.5 copy-done.4
  100.1 0.3 copy-done.6
  100.5 0.7 fusion.2
  101.2 0.7 fusion.3
  101.9 0.7 pad_maximum_fusion.12
  102.7 0.0 all-reduce.9.cloned.1.call-update
  102.7 0.0 all-reduce.13.cloned.1.call-start
  103.4 5.6 %psum.79 = f32[1]{0:T(128)} all-reduce(f32[1]{0:T(128)} %bitcast.19), channel_id=1, replica_groups=mesh['groups'=2,'atoms'=4,'kvec'=2,'rep'=2] {'kvec'}, use_global_device_ids=true, to_apply=%region_3.4 | all-reduce | flops 1 | bytes 8 | tf_op jit(solution)/shard_map/psum | solution.py:135
  109.6 16.1 %all-reduce.9.cloned.1.call-done = f32[2048,32]{0,1:T(8,128)} async-done(((f32[2048,32]{0,1:T(8,128)}), f32[2048,32]{0,1:T(8,128)}) %all-reduce.9.cloned.1.call-update) | async-done | bytes 262160 | tf_op jit(solution)/shard_map/psum | solution.py:147
  125.8 4.2 %multiply_convert_fusion.1 = bf16[2048,512]{1,0:T(8,128)(2,1)S(1)} fusion(f32[2048,512]{1,0:T(8,128)} %get-tuple-element.52, bf16[512,32]{0,1:T(8,128)(2,1)S(1)} %copy-done.15, f32[2048,32]{0,1:T(8,128)} %all-reduce.9.cloned.1.call-done, f32[]{:T(128)} %bitcast.20), kind=kOutput, calls=%fused_computation.1 | convolution fusion | flops 76677120 | bytes 6586372 | tf_op jit(solution)/shard_map/dot_general | solution.py:73
  130.0 0.0 copy-start.18
  130.0 2.3 fusion.26
  132.3 0.3 copy-done.22
  132.6 2.3 multiply_convert_fusion
  135.0 1.5 convolution_bitcast_fusion
  136.5 0.0 copy-done.2
  136.5 1.1 fusion.11
  137.6 0.0 all-reduce.13.cloned.1.call-update
  137.7 0.0 all-reduce.11.cloned.1.call-start
  137.7 20.8 %all-reduce.13.cloned.1.call-done = (f32[256,512]{0,1:T(8,128)}, f32[512,512]{1,0:T(8,128)}, f32[512,32]{0,1:T(8,128)}) async-done(((f32[256,512]{0,1:T(8,128)}, f32[512,512]{1,0:T(8,128)}, f32[512,32]{0,1:T(8,128)}), (f32[256,512]{0,1:T(8,128)}, f32[512,512]{1,0:T(8,128)}, f32[512,32]{0,1:T(8,128)})) %all-reduce.13.cloned.1.call-update) | async-done | bytes 1638416 | tf_op jit(solution)/shard_map/psum | solution.py:163
  158.5 0.0 all-reduce.11.cloned.1.call-update
  158.5 0.8 fusion.8
  159.3 3.4 %psum.86 = f32[8,512]{1,0:T(8,128)S(1)} all-reduce(f32[8,512]{1,0:T(8,128)S(1)} %fusion.8), channel_id=1, replica_groups=mesh['groups'=2,'atoms'=4,'kvec'=2,'rep'=2] {'rep'}, use_global_device_ids=true, to_apply=%region_10.11 | all-reduce | flops 4096 | bytes 32768 | tf_op jit(solution)/shard_map/psum | solution.py:163
  162.7 20.4 %psum.87 = f32[8,512]{1,0:T(8,128)} all-reduce(f32[8,512]{1,0:T(8,128)S(1)} %psum.86), channel_id=1, replica_groups=mesh['groups'=2,'atoms'=4,'kvec'=2,'rep'=2] {'atoms'}, use_global_device_ids=true, to_apply=%region_11.12 | all-reduce | flops 4096 | bytes 32768 | tf_op jit(solution)/shard_map/psum | solution.py:162
  183.0 0.7 dynamic-slice_bitcast_fusion
  183.7 51.0 %all-reduce.11.cloned.1.call-done = (f32[256,512]{0,1:T(8,128)}, f32[512,512]{1,0:T(8,128)}, f32[512,32]{0,1:T(8,128)}) async-done(((f32[256,512]{0,1:T(8,128)}, f32[512,512]{1,0:T(8,128)}, f32[512,32]{0,1:T(8,128)}), (f32[256,512]{0,1:T(8,128)}, f32[512,512]{1,0:T(8,128)}, f32[512,32]{0,1:T(8,128)})) %all-reduce.11.cloned.1.call-update) | async-done | bytes 1638416 | tf_op jit(solution)/shard_map/psum | solution.py:162
  234.7 2.1 copy.16
  236.8 2.3 copy.30
  239.0 0.6 copy.31
  (28 shorter events, 0.1 us)
Async XLA Ops:
  7.2 1.7 copy-start
  7.2 87.7 %all-reduce.7.cloned.1.call-start = ((), (), s32[]{:S(2)}) async-start(), calls=%async_computation | async-start | bytes 524288 | tf_op jit(solution)/shard_map/psum | solution.py:134
  8.8 1.7 copy-start.16
  8.8 1.7 copy-start.19
  10.6 4.2 %copy-start.17 = (bf16[512,512]{1,0:T(8,128)(2,1)S(1)}, bf16[512,512]{1,0:T(8,128)(2,1)}, u32[]{:S(2)}) copy-start(bf16[512,512]{1,0:T(8,128)(2,1)} %param.17) | copy-start | bytes 1572868
  14.8 3.8 %copy-start.20 = (bf16[2048,512]{1,0:T(8,128)(2,1)}, bf16[2048,512]{1,0:T(8,128)(2,1)S(1)}, u32[]{:S(2)}) copy-start(bf16[2048,512]{1,0:T(8,128)(2,1)S(1)} %get-tuple-element.49) | copy-start | bytes 6291460
  14.8 3.8 %copy-start.15 = (bf16[512,32]{0,1:T(8,128)(2,1)S(1)}, bf16[512,32]{0,1:T(8,128)(2,1)}, u32[]{:S(2)}) copy-start(bf16[512,32]{0,1:T(8,128)(2,1)} %param.18) | copy-start | bytes 98308
  18.5 34.3 %copy-start.1 = (bf16[2048,512]{1,0:T(8,128)(2,1)}, bf16[2048,512]{1,0:T(8,128)(2,1)S(1)}, u32[]{:S(2)}) copy-start(bf16[2048,512]{1,0:T(8,128)(2,1)S(1)} %get-tuple-element.51) | copy-start | bytes 6291460
  52.8 1.0 copy-start.3
  52.9 1.3 copy-start.5
  52.9 1.6 copy-start.7
  52.9 1.9 copy-start.9
  52.9 2.4 copy-start.11
  52.9 2.6 %copy-start.12 = (bf16[512,1024]{1,0:T(8,128)(2,1)}, bf16[512,1024]{1,0:T(8,128)(2,1)S(1)}, u32[]{:S(2)}) copy-start(bf16[512,1024]{1,0:T(8,128)(2,1)S(1)} %get-tuple-element.33) | copy-start | bytes 3145732
  56.7 69.1 %all-reduce.9.cloned.1.call-start = ((), (), s32[]{:S(2)}) async-start(), calls=%async_computation.1 | async-start | bytes 524288 | tf_op jit(solution)/shard_map/psum | solution.py:147
  94.8 4.1 %copy-start.8 = (bf16[512,1024]{1,0:T(8,128)(2,1)S(1)}, bf16[512,1024]{1,0:T(8,128)(2,1)}, u32[]{:S(2)}) copy-start(bf16[512,1024]{1,0:T(8,128)(2,1)} %copy-done.7) | copy-start | bytes 3145732
  94.8 4.1 %copy-start.10 = (bf16[512,1024]{1,0:T(8,128)(2,1)S(1)}, bf16[512,1024]{1,0:T(8,128)(2,1)}, u32[]{:S(2)}) copy-start(bf16[512,1024]{1,0:T(8,128)(2,1)} %copy-done.9) | copy-start | bytes 3145732
  98.9 1.2 copy-start.4
  98.9 1.5 copy-start.6
  102.7 55.8 %all-reduce.13.cloned.1.call-start = ((), (), s32[]{:S(2)}) async-start(), calls=%async_computation.3 | async-start | bytes 3276800 | tf_op jit(solution)/shard_map/psum | solution.py:163
  125.8 4.2 %copy-start.21 = (bf16[2048,512]{1,0:T(8,128)(2,1)S(1)}, bf16[2048,512]{1,0:T(8,128)(2,1)}, u32[]{:S(2)}) copy-start(bf16[2048,512]{1,0:T(8,128)(2,1)} %copy-done.20) | copy-start | bytes 6291460
  130.0 2.3 copy-start.18
  130.0 2.6 %copy-start.22 = (f32[2048,512]{1,0:T(8,128)S(1)}, f32[2048,512]{1,0:T(8,128)}, u32[]{:S(2)}) copy-start(f32[2048,512]{1,0:T(8,128)} %get-tuple-element.50) | copy-start | bytes 12582916
  134.9 1.6 copy-start.2
  134.9 1.6 copy-start.13
  137.7 97.0 %all-reduce.11.cloned.1.call-start = ((), (), s32[]{:S(2)}) async-start(), calls=%async_computation.2 | async-start | bytes 3276800 | tf_op jit(solution)/shard_map/psum | solution.py:162
  234.7 4.3 %copy-start.14 = (f32[512,32]{0,1:T(8,128)S(1)}, f32[512,32]{0,1:T(8,128)}, u32[]{:S(2)}) copy-start(f32[512,32]{0,1:T(8,128)} %get-tuple-element.57) | copy-start | bytes 196612
Sparse Core Ops, SparseCore 0:
  56.8 37.9 all-reduce.6
  102.8 22.9 all-reduce.8
  137.8 20.6 all-reduce.12
  161.1 73.5 all-reduce.10
